TPU v7x, 32 devices: a whole 2x2x4 slice. The times are simulated.
32 devices in a mesh: dp: 32 (over z, y, x, core).
Axes of the slice: x: 2, y: 2, z: 4, core: 2. Of those that a mesh axis runs over, the one named last changes fastest.
Arguments:
- images: bfloat16 [768, 197, 384], P('dp'), may hold values from -40 to 40
- cotangent: bfloat16 [768, 197, 384], P('dp'), may hold values from -6 to 6
- master: float32 [1774080], P('dp'), may hold values from -1.5 to 1.5
- moment_one: float32 [1774080], P('dp'), may hold values from -240 to 240
- moment_two: float32 [1774080], P('dp'), may hold values from 20 to 2000
- batch_ends: int32 [32, 3], P('dp'), may hold values from 1 to 24, as said below
Outputs:
- block_out: bfloat16 [768, 197, 384], P('dp')
- input_grad: float32 [768, 197, 384], P('dp')
- weight_grad: float32 [1774080], P('dp')
- first_moment: float32 [1774080], P('dp')
- second_moment: float32 [1774080], P('dp')
- update: float32 [1774080], P('dp')
Inputs may be any that keep to these rules, and one draw needn't show every extreme that they name: Micro-batch m of device d holds its image slots batch_ends[d, m - 1] (0 for m = 0) to batch_ends[d, m] - 1; each micro-batch holds 1 to 8 images, and some micro-batch of some device holds exactly 8. Slots from batch_ends[d, 2] on are empty.
All inputs are finite; a program needn't handle non-finite values.
Results may differ from a plain program's by a relative error of at most 0.0092.
Values may be sent and summed in bfloat16 or wider, within the bound.
A program may use at most 320 MiB of HBM per device.

v0:
```python
import jax
import jax.numpy as jnp
from jax import lax
from jax.sharding import PartitionSpec as P

D = 384
FF = 1536
HEADS = 6
HEAD_DIM = 64
TOK_IMG = 197
MB = 3
STEP = 10


beta_one = 0.9
beta_two = 0.999
learn_rate = 0.01
decay_rate = 0.05
adam_eps = 1e-08
norm_eps = 1e-06


def layer_norm(values, gain_vec, shift_vec):
    centre = jnp.mean(values, axis=-1, keepdims=True)
    centered = values - centre
    spread = jnp.mean(centered * centered, axis=-1, keepdims=True)
    return centered * lax.rsqrt(spread + norm_eps) * gain_vec + shift_vec


def gelu_exact(values):
    return jax.nn.gelu(values, approximate=False)


def unpack(flat_vec):
    lengths = [3 * D * D, D * D, D * FF, FF * D, D, D, D, D, D, D, D, D, FF]
    pieces = []
    offset = 0
    for length_one in lengths:
        pieces.append(flat_vec[offset : offset + length_one])
        offset = offset + length_one
    shapes = [(D, 3 * D), (D, D), (D, FF), (FF, D)]
    return [pieces[number].reshape(shapes[number]) for number in range(4)] + pieces[4:]


def forward_pass(unpacked, batch_images, live_mask):
    w_qkv, w_out, w_up, w_down = unpacked[:4]
    (
        gain_one,
        shift_one,
        gain_two,
        shift_two,
        bias_query,
        bias_value,
        bias_out,
        bias_down,
        bias_up,
    ) = [member.astype(jnp.float32) for member in unpacked[4:]]
    count_img = batch_images.shape[0]
    rows_in = batch_images.reshape(count_img * TOK_IMG, D).astype(jnp.float32)
    normed_one, back_one = jax.vjp(layer_norm, rows_in, gain_one, shift_one)
    normed_one_low = normed_one.astype(jnp.bfloat16)
    bias_qkv = jnp.concatenate([bias_query, jnp.zeros_like(bias_query), bias_value])
    qkv_low = (
        jnp.dot(normed_one_low, w_qkv, preferred_element_type=jnp.float32) + bias_qkv
    ).astype(jnp.bfloat16)
    qkv_heads = qkv_low.reshape(count_img, TOK_IMG, 3, HEADS, HEAD_DIM).transpose(2, 0, 3, 1, 4)
    query_heads = qkv_heads[0]
    key_heads = qkv_heads[1]
    value_heads = qkv_heads[2]
    score_scale = HEAD_DIM ** (-0.5)
    scores = (
        jnp.einsum("nhqe,nhke->nhqk", query_heads, key_heads, preferred_element_type=jnp.float32)
        * score_scale
    )
    row_top = jnp.max(scores, axis=-1, keepdims=True)
    shifted_exp = jnp.exp(scores - row_top)
    totals = jnp.sum(shifted_exp, axis=-1, keepdims=True)
    soft_probs = shifted_exp / totals
    log_total = row_top + jnp.log(totals)
    mixed_heads = jnp.einsum(
        "nhqk,nhke->nhqe",
        soft_probs.astype(jnp.bfloat16),
        value_heads,
        preferred_element_type=jnp.float32,
    )
    mixed_low = (
        mixed_heads.astype(jnp.bfloat16).transpose(0, 2, 1, 3).reshape(count_img * TOK_IMG, D)
    )
    middle = rows_in + jnp.dot(mixed_low, w_out, preferred_element_type=jnp.float32) + bias_out
    normed_two, back_two = jax.vjp(layer_norm, middle, gain_two, shift_two)
    normed_two_low = normed_two.astype(jnp.bfloat16)
    hidden_pre = jnp.dot(normed_two_low, w_up, preferred_element_type=jnp.float32) + bias_up
    active, back_gelu = jax.vjp(gelu_exact, hidden_pre)
    active_low = active.astype(jnp.bfloat16)
    result = middle + jnp.dot(active_low, w_down, preferred_element_type=jnp.float32) + bias_down
    result = result.reshape(batch_images.shape) * live_mask[:, None, None]
    kept_state = (
        normed_one_low,
        back_one,
        query_heads,
        key_heads,
        value_heads,
        log_total,
        mixed_low,
        back_two,
        normed_two_low,
        back_gelu,
        active_low,
    )
    return (result, kept_state)


def backward_pass(unpacked, kept_state, upstream_block, live_mask):
    w_qkv, w_out, w_up, w_down = unpacked[:4]
    (
        normed_one_low,
        back_one,
        query_heads,
        key_heads,
        value_heads,
        log_total,
        mixed_low,
        back_two,
        normed_two_low,
        back_gelu,
        active_low,
    ) = kept_state
    count_img = upstream_block.shape[0]
    upstream = (upstream_block * live_mask[:, None, None].astype(jnp.bfloat16)).reshape(
        count_img * TOK_IMG, D
    )
    upstream_wide = upstream.astype(jnp.float32)
    grad_down = jnp.dot(active_low.T, upstream, preferred_element_type=jnp.float32)
    grad_bias_down = jnp.sum(upstream_wide, axis=0)
    grad_active = jnp.dot(upstream, w_down.T, preferred_element_type=jnp.float32)
    grad_pre = back_gelu(grad_active)[0].astype(jnp.bfloat16)
    grad_up = jnp.dot(normed_two_low.T, grad_pre, preferred_element_type=jnp.float32)
    grad_bias_up = jnp.sum(grad_pre.astype(jnp.float32), axis=0)
    grad_normed_two = jnp.dot(grad_pre, w_up.T, preferred_element_type=jnp.float32)
    grad_middle_norm, grad_gain_two, grad_shift_two = back_two(grad_normed_two)
    grad_middle = upstream_wide + grad_middle_norm
    grad_branch = grad_middle.astype(jnp.bfloat16)
    grad_out = jnp.dot(mixed_low.T, grad_branch, preferred_element_type=jnp.float32)
    grad_bias_out = jnp.sum(grad_branch.astype(jnp.float32), axis=0)
    grad_mixed = jnp.dot(grad_branch, w_out.T, preferred_element_type=jnp.float32).astype(
        jnp.bfloat16
    )
    grad_mixed = grad_mixed.reshape(count_img, TOK_IMG, HEADS, HEAD_DIM).transpose(0, 2, 1, 3)
    score_scale = HEAD_DIM ** (-0.5)
    scores = (
        jnp.einsum("nhqe,nhke->nhqk", query_heads, key_heads, preferred_element_type=jnp.float32)
        * score_scale
    )
    soft_probs = jnp.exp(scores - log_total)
    grad_value = jnp.einsum(
        "nhqk,nhqe->nhke",
        soft_probs.astype(jnp.bfloat16),
        grad_mixed,
        preferred_element_type=jnp.float32,
    )
    grad_probs = jnp.einsum(
        "nhqe,nhke->nhqk", grad_mixed, value_heads, preferred_element_type=jnp.float32
    )
    row_dot = jnp.sum(soft_probs * grad_probs, axis=-1, keepdims=True)
    grad_scores = (soft_probs * (grad_probs - row_dot)).astype(jnp.bfloat16)
    grad_query = (
        jnp.einsum("nhqk,nhke->nhqe", grad_scores, key_heads, preferred_element_type=jnp.float32)
        * score_scale
    )
    grad_key = (
        jnp.einsum("nhqk,nhqe->nhke", grad_scores, query_heads, preferred_element_type=jnp.float32)
        * score_scale
    )
    grad_stack = jnp.stack([grad_query, grad_key, grad_value], axis=0).astype(jnp.bfloat16)
    grad_qkv = grad_stack.transpose(1, 3, 0, 2, 4).reshape(count_img * TOK_IMG, 3 * D)
    grad_in_proj = jnp.dot(normed_one_low.T, grad_qkv, preferred_element_type=jnp.float32)
    qkv_sums = jnp.sum(grad_qkv.astype(jnp.float32), axis=0)
    grad_normed_one = jnp.dot(grad_qkv, w_qkv.T, preferred_element_type=jnp.float32)
    grad_rows_norm, grad_gain_one, grad_shift_one = back_one(grad_normed_one)
    grad_rows = grad_middle + grad_rows_norm
    grad_parts = (
        grad_in_proj,
        grad_out,
        grad_up,
        grad_down,
        grad_gain_one,
        grad_shift_one,
        grad_gain_two,
        grad_shift_two,
        qkv_sums[:D],
        qkv_sums[2 * D :],
        grad_bias_out,
        grad_bias_down,
        grad_bias_up,
    )
    return (grad_parts, grad_rows.reshape(upstream_block.shape))


def body(images, cotangent, master, moment_one, moment_two, batch_ends):
    limits = batch_ends[0]
    firsts = jnp.concatenate([jnp.zeros((1,), jnp.int32), limits[:-1]])
    capacity = images.shape[0] // MB
    master_low = master.astype(jnp.bfloat16)
    block_out = jnp.zeros(images.shape, jnp.bfloat16)
    input_grad = jnp.zeros(images.shape, jnp.float32)
    grad_total = None
    for micro_step in range(MB):
        offset = firsts[micro_step]
        live_mask = (jnp.arange(capacity, dtype=jnp.int32) < limits[micro_step] - offset).astype(
            jnp.float32
        )
        batch_images = lax.dynamic_slice_in_dim(images, offset, capacity, 0)
        upstream_block = lax.dynamic_slice_in_dim(cotangent, offset, capacity, 0)
        forward_unpacked = unpack(lax.all_gather(master_low, "dp", axis=0, tiled=True))
        result, kept_state = forward_pass(forward_unpacked, batch_images, live_mask)
        backward_unpacked = unpack(lax.all_gather(master_low, "dp", axis=0, tiled=True))
        grad_parts, grad_rows = backward_pass(
            backward_unpacked, kept_state, upstream_block, live_mask
        )
        if grad_total is None:
            grad_total = grad_parts
        else:
            grad_total = jax.tree.map(lambda left, right: left + right, grad_total, grad_parts)
        keep_rows = live_mask[:, None, None] > 0.5
        current_out = lax.dynamic_slice_in_dim(block_out, offset, capacity, 0)
        block_out = lax.dynamic_update_slice_in_dim(
            block_out, jnp.where(keep_rows, result.astype(jnp.bfloat16), current_out), offset, 0
        )
        current_grad = lax.dynamic_slice_in_dim(input_grad, offset, capacity, 0)
        input_grad = lax.dynamic_update_slice_in_dim(
            input_grad, jnp.where(keep_rows, grad_rows, current_grad), offset, 0
        )
    grad_flat = jnp.concatenate([member.reshape(-1) for member in grad_total])
    weight_grad = lax.psum_scatter(grad_flat, "dp", scatter_dimension=0, tiled=True)
    first_moment = beta_one * moment_one + (1.0 - beta_one) * weight_grad
    second_moment = beta_two * moment_two + (1.0 - beta_two) * weight_grad * weight_grad
    corrected_one = first_moment / (1.0 - beta_one**STEP)
    corrected_two = second_moment / (1.0 - beta_two**STEP)
    update = -learn_rate * (
        corrected_one / (jnp.sqrt(corrected_two) + adam_eps) + decay_rate * master
    )
    return (block_out, input_grad, weight_grad, first_moment, second_moment, update)


def solution(mesh):
    return jax.shard_map(
        body,
        mesh=mesh,
        in_specs=(
            P("dp", None, None),
            P("dp", None, None),
            P("dp"),
            P("dp"),
            P("dp"),
            P("dp", None),
        ),
        out_specs=(P("dp", None, None), P("dp", None, None), P("dp"), P("dp"), P("dp"), P("dp")),
        check_vma=False,
    )
```

profile of v0, /device:TPU:0, one launch (start us, length us, event | category | flops | bytes accessed | tf_op | source)
XLA Modules:
  0.0 989.2 jit_solution(15958010743755780550)
XLA Ops:
  20.8 8.0 convert_reduce_fusion.6
  29.7 7.1 multiply_reduce_fusion.19
  46.9 5.8 dynamic-slice_convert_fusion
  56.6 4.5 copy.142
  73.8 82.1 %all-reduce.7.cloned.1.call-done = bf16[1774080]{0:T(1024)(128)(2,1)} async-done(((bf16[1774080]{0:T(1024)(128)(2,1)}), bf16[1774080]{0:T(1024)(128)(2,1)}) %all-reduce.7.cloned.1.call-update) | async-done | bytes 3548176
  160.5 6.0 fusion.22
  166.6 12.1 %reshape.581 = bf16[8,197,3,6,64]{4,3,2,1,0:T(8,128)(2,1)} reshape(bf16[1576,1152]{1,0:T(8,128)(2,1)} %fusion.22) | data formatting | bytes 7262208 | tf_op jit(solution)/shard_map/reshape | solution.py:66
  178.7 11.5 %copy.155 = bf16[8,197,3,6,64]{1,4,3,0,2:T(8,128)(2,1)} copy(bf16[8,197,3,6,64]{4,3,2,1,0:T(8,128)(2,1)} %reshape.581) | data formatting | bytes 7262208 | tf_op jit(solution)/shard_map/reshape | solution.py:66
  197.4 5.0 fusion.73
  202.4 4.2 fusion.21
  206.6 11.8 %reshape.580 = bf16[8,197,3,6,64]{4,3,2,1,0:T(8,128)(2,1)} reshape(bf16[1576,1152]{1,0:T(8,128)(2,1)} %fusion.21) | data formatting | bytes 7262208 | tf_op jit(solution)/shard_map/reshape | solution.py:66
  218.4 11.4 %copy.147 = bf16[8,197,3,6,64]{1,4,3,0,2:T(8,128)(2,1)} copy(bf16[8,197,3,6,64]{4,3,2,1,0:T(8,128)(2,1)} %reshape.580) | data formatting | bytes 7262208 | tf_op jit(solution)/shard_map/reshape | solution.py:66
  236.9 5.0 fusion.72
  242.0 4.2 fusion.23
  246.2 11.8 %reshape.582 = bf16[8,197,3,6,64]{4,3,2,1,0:T(8,128)(2,1)} reshape(bf16[1576,1152]{1,0:T(8,128)(2,1)} %fusion.23) | data formatting | bytes 7262208 | tf_op jit(solution)/shard_map/reshape | solution.py:66
  257.9 11.4 %copy.163 = bf16[8,197,3,6,64]{1,4,3,0,2:T(8,128)(2,1)} copy(bf16[8,197,3,6,64]{4,3,2,1,0:T(8,128)(2,1)} %reshape.582) | data formatting | bytes 7262208 | tf_op jit(solution)/shard_map/reshape | solution.py:66
  276.6 4.9 fusion.74
  290.8 4.1 reshape.551
  298.2 25.6 %multiply_convert_fusion.5 = (bf16[1576,1536]{1,0:T(8,128)(2,1)}, f32[1576,1536]{1,0:T(8,128)S(1)}, f32[1576,1536]{1,0:T(8,128)}) fusion(f32[1536]{0:T(1024)S(1)} %slice_convert_fusion.1, bf16[384,1536]{1,0:T(8,128)(2,1)S(1)} %copy-done.72, f32[1576,384]{1,0:T(8,128)S(1)} %get-tuple-element.142, f32[384]{0:T(512)S(1)} %get-tuple-element.99, ...), kind=kOutput, calls=%fused_computation.56 | convolution fusion | flops 2021919744 | bytes 27829568 | tf_op jit(solution)/shard_map/dot_general | solution.py:92
  323.8 8.8 convert_reduce_fusion.2
  336.6 4.2 fusion.145
  358.8 25.8 %multiply_convert_fusion.3 = (bf16[1576,1536]{1,0:T(8,128)(2,1)}, f32[1576,1536]{1,0:T(8,128)}, f32[1576,1536]{1,0:T(8,128)}) fusion(f32[1536]{0:T(1024)S(1)} %slice_convert_fusion.1, bf16[384,1536]{1,0:T(8,128)(2,1)S(1)} %copy-done.73, f32[1576,384]{1,0:T(8,128)S(1)} %get-tuple-element.152, f32[1576]{0:T(1024)S(1)} %fusion.113, ...), kind=kOutput, calls=%fused_computation.30 | convolution fusion | flops 2021919744 | bytes 27829568 | tf_op jit(solution)/shard_map/dot_general | solution.py:92
  384.6 25.8 %multiply_convert_fusion.4 = (bf16[1576,1536]{1,0:T(8,128)(2,1)}, f32[1576,1536]{1,0:T(8,128)}, f32[1576,1536]{1,0:T(8,128)}) fusion(f32[1536]{0:T(1024)S(1)} %slice_convert_fusion.1, bf16[384,1536]{1,0:T(8,128)(2,1)S(1)} %copy-done.73, f32[1576,384]{1,0:T(8,128)S(1)} %get-tuple-element.147, f32[1576]{0:T(1024)S(1)} %fusion.112, ...), kind=kOutput, calls=%fused_computation.43 | convolution fusion | flops 2021919744 | bytes 27829568 | tf_op jit(solution)/shard_map/dot_general | solution.py:92
  410.4 10.2 %convert_reduce_fusion.1 = (f32[1536]{0:T(1024)}, bf16[1576,1536]{1,0:T(8,128)(2,1)S(1)}) fusion(f32[1576,1536]{1,0:T(8,128)} %get-tuple-element.85, f32[1576,1536]{1,0:T(8,128)} %get-tuple-element.148, bf16[1576,384]{1,0:T(8,128)(2,1)S(1)} %copy-done.34, bf16[1536,384]{1,0:T(8,128)(2,1)S(1)} %copy-done.69), kind=kOutput, calls=%fused_computation.25 | convolution fusion | flops 1897855488 | bytes 26603520 | tf_op jit(solution)/shard_map/dot_general | solution.py:135
  423.5 11.2 %convert_reduce_fusion = (f32[1536]{0:T(1024)}, bf16[1576,1536]{1,0:T(8,128)(2,1)S(1)}) fusion(f32[1576,1536]{1,0:T(8,128)} %get-tuple-element.83, f32[1576,1536]{1,0:T(8,128)} %get-tuple-element.153, bf16[1576,384]{1,0:T(8,128)(2,1)S(1)} %copy-done.30, bf16[1536,384]{1,0:T(8,128)(2,1)S(1)} %copy-done.69), kind=kOutput, calls=%fused_computation.24 | convolution fusion | flops 1897855488 | bytes 26603520 | tf_op jit(solution)/shard_map/dot_general | solution.py:135
  434.7 6.4 multiply_reduce_fusion.6
  441.3 9.6 fusion.132
  463.7 5.1 reshape.564
  468.8 7.6 fusion.66
  476.3 8.8 multiply_reduce_fusion.1
  485.2 11.6 %multiply_convert_fusion.1 = bf16[8,6,197,197]{2,3,1,0:T(8,128)(2,1)} fusion(f32[8,6,197,197]{2,3,1,0:T(8,128)} %get-tuple-element.158, f32[8,6,197,197]{2,3,1,0:T(8,128)} %copy-done.2, f32[8,6,197]{2,1,0:T(8,128)S(1)} %get-tuple-element.157, f32[8,6,197]{2,1,0:T(8,128)S(1)} %copy-done.76), kind=kLoop, calls=%fused_computation.6 | loop fusion | flops 9314160 | bytes 18703968 | tf_op jit(solution)/shard_map/convert_element_type | solution.py:165
  496.7 5.9 fusion.78
  508.8 4.7 reshape.560
  513.4 7.6 fusion.69
  521.0 9.1 multiply_reduce_fusion.2
  530.1 11.6 %multiply_convert_fusion.2 = bf16[8,6,197,197]{2,3,1,0:T(8,128)(2,1)} fusion(f32[8,6,197,197]{2,3,1,0:T(8,128)} %get-tuple-element.160, f32[8,6,197,197]{2,3,1,0:T(8,128)} %copy-done.1, f32[8,6,197]{2,1,0:T(8,128)S(1)} %get-tuple-element.159, f32[8,6,197]{2,1,0:T(8,128)S(1)} %copy-done.75), kind=kLoop, calls=%fused_computation.9 | loop fusion | flops 9314160 | bytes 18703968 | tf_op jit(solution)/shard_map/convert_element_type | solution.py:165
  541.6 5.9 fusion.76
  557.5 4.7 reshape.568
  562.2 7.6 fusion.63
  569.7 8.8 multiply_reduce_fusion
  578.5 11.6 %multiply_convert_fusion = bf16[8,6,197,197]{2,3,1,0:T(8,128)(2,1)} fusion(f32[8,6,197,197]{2,3,1,0:T(8,128)} %get-tuple-element.156, f32[8,6,197,197]{2,3,1,0:T(8,128)} %copy-done, f32[8,6,197]{2,1,0:T(8,128)S(1)} %get-tuple-element.155, f32[8,6,197]{2,1,0:T(8,128)S(1)} %copy-done.74), kind=kLoop, calls=%fused_computation.3 | loop fusion | flops 9314160 | bytes 18703968 | tf_op jit(solution)/shard_map/convert_element_type | solution.py:165
  590.1 5.8 fusion.80
  617.9 7.4 fusion.151
  625.3 6.7 fusion.45
  632.0 4.2 fusion.47
  647.3 6.8 fusion.46
  654.1 5.0 convolution_add_fusion.12
  659.1 7.0 convolution_add_fusion.11
  669.3 5.9 convolution_add_fusion.14
  675.2 4.9 convolution_add_fusion.13
  689.5 4.5 copy.196
  701.7 5.5 copy.181
  707.2 9.3 reshape.565
  716.5 6.2 fusion.148
  724.4 5.5 copy.173
  729.9 8.8 reshape.561
  738.7 6.1 fusion.146
  751.1 7.8 copy.189
  759.0 9.0 reshape.569
  768.0 11.2 %multiply_reduce_fusion.9 = (f32[384]{0:T(512)S(1)}, f32[1576]{0:T(1024)S(1)}, f32[384]{0:T(512)S(1)}, f32[384]{0:T(512)S(1)}, f32[1576]{0:T(1024)S(1)}, /*index...) fusion(f32[1576,384]{1,0:T(8,128)S(1)} %copy-done.14, ...), kind=kOutput, calls=%fused_computation.152 | convolution fusion | flops 1408861440 | bytes 19107744 | tf_op jit(solution)/shard_map/dot_general | solution.py:178
  787.7 9.5 fusion.131
  824.8 4.1 add_add_fusion.10
  844.4 4.3 copy.197
  848.7 131.4 %all-reduce.9.cloned.1.call-done = f32[1774080]{0:T(1024)} async-done(((f32[1774080]{0:T(1024)}), f32[1774080]{0:T(1024)}) %all-reduce.9.cloned.1.call-update) | async-done | bytes 7096336
  (488 shorter events, 241.5 us)
Async XLA Ops:
  7.2 148.7 %all-reduce.7.cloned.1.call-start = ((), (), s32[]{:S(2)}) async-start(), calls=%async_computation | async-start | bytes 7098368
  13.1 967.0 %all-reduce.9.cloned.1.call-start = ((), (), s32[]{:S(2)}) async-start(), calls=%async_computation.1 | async-start | bytes 14196736
  29.0 213.0 %copy-start.111 = (f32[1576]{0:T(1024)}, f32[1576]{0:T(1024)S(1)}, u32[]{:S(2)}) copy-start(f32[1576]{0:T(1024)S(1)} %div.168) | copy-start | bytes 18916
  29.1 10.6 %copy-start.77 = (f32[8,197]{0,1:T(8,128)}, f32[8,197]{0,1:T(8,128)S(1)}, u32[]{:S(2)}) copy-start(f32[8,197]{0,1:T(8,128)S(1)} %copy.160) | copy-start | bytes 18916
  29.3 131.3 %copy-start.113 = (f32[1576]{0:T(1024)}, f32[1576]{0:T(1024)S(1)}, u32[]{:S(2)}) copy-start(f32[1576]{0:T(1024)S(1)} %div.161) | copy-start | bytes 18916
  29.4 10.3 %copy-start.79 = (f32[8,197]{0,1:T(8,128)}, f32[8,197]{0,1:T(8,128)S(1)}, u32[]{:S(2)}) copy-start(f32[8,197]{0,1:T(8,128)S(1)} %copy.152) | copy-start | bytes 18916
  29.6 172.8 %copy-start.115 = (f32[1576]{0:T(1024)}, f32[1576]{0:T(1024)S(1)}, u32[]{:S(2)}) copy-start(f32[1576]{0:T(1024)S(1)} %div.154) | copy-start | bytes 18916
  29.7 10.0 %copy-start.81 = (f32[8,197]{0,1:T(8,128)}, f32[8,197]{0,1:T(8,128)S(1)}, u32[]{:S(2)}) copy-start(f32[8,197]{0,1:T(8,128)S(1)} %copy.144) | copy-start | bytes 18916
  37.1 165.3 %copy-start.117 = (f32[1576]{0:T(1024)}, f32[1576]{0:T(1024)S(1)}, u32[]{:S(2)}) copy-start(f32[1576]{0:T(1024)S(1)} %rsqrt.69) | copy-start | bytes 18916
  37.2 123.3 %copy-start.119 = (f32[1576]{0:T(1024)}, f32[1576]{0:T(1024)S(1)}, u32[]{:S(2)}) copy-start(f32[1576]{0:T(1024)S(1)} %rsqrt.71) | copy-start | bytes 18916
  37.4 204.6 %copy-start.121 = (f32[1576]{0:T(1024)}, f32[1576]{0:T(1024)S(1)}, u32[]{:S(2)}) copy-start(f32[1576]{0:T(1024)S(1)} %rsqrt.73) | copy-start | bytes 18916
  56.6 185.3 %copy-start.13 = (f32[1576,384]{1,0:T(8,128)}, f32[1576,384]{1,0:T(8,128)S(1)}, u32[]{:S(2)}) copy-start(f32[1576,384]{1,0:T(8,128)S(1)} %reshape.577) | copy-start | bytes 7262212
  160.5 81.5 %copy-start.125 = (f32[384]{0:T(512)}, f32[384]{0:T(512)S(1)}, u32[]{:S(2)}) copy-start(f32[384]{0:T(512)S(1)} %get-tuple-element.105) | copy-start | bytes 4612
  160.5 81.5 %copy-start.135 = (f32[384]{0:T(512)}, f32[384]{0:T(512)S(1)}, u32[]{:S(2)}) copy-start(f32[384]{0:T(512)S(1)} %get-tuple-element.104) | copy-start | bytes 4612
  160.5 224.0 %copy-start.141 = (f32[384]{0:T(512)}, f32[384]{0:T(512)S(1)}, u32[]{:S(2)}) copy-start(f32[384]{0:T(512)S(1)} %get-tuple-element.99) | copy-start | bytes 4612
  281.6 73.2 %copy-start.22 = (bf16[384,384]{1,0:T(8,128)(2,1)}, bf16[384,384]{1,0:T(8,128)(2,1)S(1)}, u32[]{:S(2)}) copy-start(bf16[384,384]{1,0:T(8,128)(2,1)S(1)} %slice.199) | copy-start | bytes 884740
  287.1 7.8 copy-start.16
  297.6 35.0 %copy-start.7 = (f32[1576,384]{1,0:T(8,128)}, f32[1576,384]{1,0:T(8,128)S(1)}, u32[]{:S(2)}) copy-start(f32[1576,384]{1,0:T(8,128)S(1)} %get-tuple-element.142) | copy-start | bytes 7262212
  297.6 35.0 %copy-start.91 = (f32[1576]{0:T(1024)}, f32[1576]{0:T(1024)S(1)}, u32[]{:S(2)}) copy-start(f32[1576]{0:T(1024)S(1)} %broadcast_multiply_fusion.2) | copy-start | bytes 18916
  298.2 25.6 %copy-start.99 = (f32[1576]{0:T(1024)}, f32[1576]{0:T(1024)S(1)}, u32[]{:S(2)}) copy-start(f32[1576]{0:T(1024)S(1)} %multiply_reduce_fusion.22) | copy-start | bytes 18916
  298.2 34.4 %copy-start.123 = (f32[1576]{0:T(1024)}, f32[1576]{0:T(1024)S(1)}, u32[]{:S(2)}) copy-start(f32[1576]{0:T(1024)S(1)} %fusion.111) | copy-start | bytes 18916
  298.2 25.6 %copy-start.33 = (bf16[1576,384]{1,0:T(8,128)(2,1)S(1)}, bf16[1576,384]{1,0:T(8,128)(2,1)}, u32[]{:S(2)}) copy-start(bf16[1576,384]{1,0:T(8,128)(2,1)} %reshape.559) | copy-start | bytes 3631108
  298.2 25.6 %copy-start.68 = (bf16[1536,384]{1,0:T(8,128)(2,1)S(1)}, bf16[1536,384]{1,0:T(8,128)(2,1)}, u32[]{:S(2)}) copy-start(bf16[1536,384]{1,0:T(8,128)(2,1)} %slice.207) | copy-start | bytes 3538948
  348.7 9.4 copy-start.101
  358.1 76.5 %copy-start.10 = (f32[1576,384]{1,0:T(8,128)}, f32[1576,384]{1,0:T(8,128)S(1)}, u32[]{:S(2)}) copy-start(f32[1576,384]{1,0:T(8,128)S(1)} %get-tuple-element.152) | copy-start | bytes 7262212
  358.7 25.8 %copy-start.103 = (f32[1576]{0:T(1024)}, f32[1576]{0:T(1024)S(1)}, u32[]{:S(2)}) copy-start(f32[1576]{0:T(1024)S(1)} %multiply_reduce_fusion.18) | copy-start | bytes 18916
  384.5 25.8 %copy-start.34 = (bf16[1576,384]{1,0:T(8,128)(2,1)S(1)}, bf16[1576,384]{1,0:T(8,128)(2,1)}, u32[]{:S(2)}) copy-start(bf16[1576,384]{1,0:T(8,128)(2,1)} %reshape.563) | copy-start | bytes 3631108
  384.6 25.8 %copy-start.69 = (bf16[1536,384]{1,0:T(8,128)(2,1)S(1)}, bf16[1536,384]{1,0:T(8,128)(2,1)}, u32[]{:S(2)}) copy-start(bf16[1536,384]{1,0:T(8,128)(2,1)} %slice.207) | copy-start | bytes 3538948
  423.4 11.2 %copy-start.61 = (f32[1576,384]{1,0:T(8,128)}, f32[1576,384]{1,0:T(8,128)S(1)}, u32[]{:S(2)}) copy-start(f32[1576,384]{1,0:T(8,128)S(1)} %fusion.147) | copy-start | bytes 7262212
  423.5 11.2 %copy-start.8 = (f32[1576,384]{1,0:T(8,128)S(1)}, f32[1576,384]{1,0:T(8,128)}, u32[]{:S(2)}) copy-start(f32[1576,384]{1,0:T(8,128)} %copy-done.7) | copy-start | bytes 7262212
  423.5 11.2 %copy-start.60 = (f32[1576,384]{1,0:T(8,128)S(1)}, f32[1576,384]{1,0:T(8,128)}, u32[]{:S(2)}) copy-start(f32[1576,384]{1,0:T(8,128)} %fusion.145) | copy-start | bytes 7262212
  423.5 11.2 %copy-start.92 = (f32[1576]{0:T(1024)S(1)}, f32[1576]{0:T(1024)}, u32[]{:S(2)}) copy-start(f32[1576]{0:T(1024)} %copy-done.91) | copy-start | bytes 18916
  423.5 11.2 %copy-start.124 = (f32[1576]{0:T(1024)S(1)}, f32[1576]{0:T(1024)}, u32[]{:S(2)}) copy-start(f32[1576]{0:T(1024)} %copy-done.123) | copy-start | bytes 18916
  461.1 7.7 copy-start.76
  468.8 7.6 copy-start.25
  513.4 7.6 copy-start.26
  562.2 7.6 copy-start.27
  617.9 7.4 copy-start.143
  617.9 14.1 %slice-start.1 = ((s8[4841472]{0:T(1024)(128)(4,1)}), s8[4194304]{0:T(1024)(128)(4,1)S(1)}, s32[]{:S(2)}) async-start(s8[4841472]{0:T(1024)(128)(4,1)} %bitcast.216), calls=%async_computation.3 | async-start | bytes 8388608
  707.2 9.3 copy-start.85
  758.9 9.0 copy-start.14
  758.9 9.0 copy-start.112
  758.9 9.0 copy-start.114
  758.9 9.0 copy-start.116
  758.9 9.0 copy-start.118
  758.9 9.0 copy-start.120
  758.9 9.0 copy-start.122
  768.0 11.2 %copy-start.106 = (f32[1576]{0:T(1024)S(1)}, f32[1576]{0:T(1024)}, u32[]{:S(2)}) copy-start(f32[1576]{0:T(1024)} %copy-done.105) | copy-start | bytes 18916
  768.0 11.2 %copy-start.108 = (f32[1576]{0:T(1024)S(1)}, f32[1576]{0:T(1024)}, u32[]{:S(2)}) copy-start(f32[1576]{0:T(1024)} %copy-done.107) | copy-start | bytes 18916
  768.0 11.3 %copy-start.110 = (f32[1576]{0:T(1024)S(1)}, f32[1576]{0:T(1024)}, u32[]{:S(2)}) copy-start(f32[1576]{0:T(1024)} %copy-done.109) | copy-start | bytes 18916
  768.0 11.3 %copy-start.56 = (bf16[1576,1152]{0,1:T(8,128)(2,1)S(1)}, bf16[1576,1152]{0,1:T(8,128)(2,1)}, u32[]{:S(2)}) copy-start(bf16[1576,1152]{0,1:T(8,128)(2,1)} %reshape.565) | copy-start | bytes 10893316
  768.0 11.3 %copy-start.66 = (bf16[1576,384]{1,0:T(8,128)(2,1)S(1)}, bf16[1576,384]{1,0:T(8,128)(2,1)}, u32[]{:S(2)}) copy-start(bf16[1576,384]{1,0:T(8,128)(2,1)} %convert_element_type.400) | copy-start | bytes 3631108
  768.0 11.3 %copy-start.154 = (f32[384,1152]{1,0:T(8,128)S(1)}, f32[384,1152]{1,0:T(8,128)}, u32[]{:S(2)}) copy-start(f32[384,1152]{1,0:T(8,128)} %fusion.149) | copy-start | bytes 5308420
  802.7 9.5 copy-start.130
  802.7 9.5 copy-start.131
  802.7 10.8 %copy-start.127 = (f32[384]{0:T(512)S(1)}, f32[384]{0:T(512)}, u32[]{:S(2)}) copy-start(f32[384]{0:T(512)} %get-tuple-element.56) | copy-start | bytes 4612
  802.7 10.8 %copy-start.128 = (f32[384]{0:T(512)S(1)}, f32[384]{0:T(512)}, u32[]{:S(2)}) copy-start(f32[384]{0:T(512)} %get-tuple-element.91) | copy-start | bytes 4612
  802.7 10.7 %copy-start.129 = (f32[384]{0:T(512)S(1)}, f32[384]{0:T(512)}, u32[]{:S(2)}) copy-start(f32[384]{0:T(512)} %get-tuple-element.93) | copy-start | bytes 4612
  802.7 12.0 %copy-start.132 = (f32[1536]{0:T(1024)S(1)}, f32[1536]{0:T(1024)}, u32[]{:S(2)}) copy-start(f32[1536]{0:T(1024)} %get-tuple-element.164) | copy-start | bytes 18436
  802.7 12.0 %copy-start.133 = (f32[1536]{0:T(1024)S(1)}, f32[1536]{0:T(1024)}, u32[]{:S(2)}) copy-start(f32[1536]{0:T(1024)} %get-tuple-element.166) | copy-start | bytes 18436
  802.7 12.0 %copy-start.134 = (f32[1536]{0:T(1024)S(1)}, f32[1536]{0:T(1024)}, u32[]{:S(2)}) copy-start(f32[1536]{0:T(1024)} %get-tuple-element.162) | copy-start | bytes 18436
  844.4 135.7 %copy-start.83 = (f32[55440]{0:T(1024)S(1)}, f32[55440]{0:T(1024)}, u32[]{:S(2)}) copy-start(f32[55440]{0:T(1024)} %param.8) | copy-start | bytes 665284
  844.4 135.7 %copy-start.89 = (f32[55440]{0:T(1024)S(1)}, f32[55440]{0:T(1024)}, u32[]{:S(2)}) copy-start(f32[55440]{0:T(1024)} %param.10) | copy-start | bytes 665284
  844.4 135.7 %copy-start.90 = (f32[55440]{0:T(1024)S(1)}, f32[55440]{0:T(1024)}, u32[]{:S(2)}) copy-start(f32[55440]{0:T(1024)} %param.9) | copy-start | bytes 665284
  (98 other events, 394.7 us)
Sparse Core Ops, SparseCore 0:
  14.2 141.6 all-reduce.6
  815.5 164.5 all-reduce.8
where the time goes:
time: 1000 us; the launch traced here: 989 us
  matrix products  341 us (34%)
  local copies, waits for them, and re-layouts  272 us (27%)
  waiting for transfers between devices  214 us (21%)
  other arithmetic  140 us (14%)
  between operations  22.3 us (2%)
    unnamed x4, waiting for transfers between devices  214 us
    dot_general x3, matrix products, forward_pass(): jnp.dot(normed_two_low, w_up, preferred_element_type=jnp.float32) + bias_up  77.1 us
    reshape x6, local copies, waits for them, and re-layouts, forward_pass(): qkv_low.reshape(count_img, TOK_IMG, 3, HEADS, HEAD_DIM)  70 us
    convert_element_type x3, other arithmetic, backward_pass(): grad_scores = (soft_probs * (grad_probs - row_dot)).astype(jnp.bfloat16)  34.7 us
    unnamed x328, local copies, waits for them, and re-layouts  31.4 us
    dot_general x3, matrix products, backward_pass(): jnp.dot(upstream, w_down.T, preferred_element_type=jnp.float32)  30.2 us
    reshape x3, local copies, waits for them, and re-layouts, backward_pass(): grad_stack.transpose(1, 3, 0, 2, 4).reshape(count_img * TOK_IMG, 3 * D)  27.1 us
    dot_general x3, matrix products, backward_pass(): jnp.einsum('nhqe,nhke->nhqk', grad_mixed, value_heads, preferred_element_...  26.7 us
  transfers between devices with their start and end apart: 2, of which 2 were waited for; matrix products, arithmetic and copies ran while one was open for 8% of the time, Pallas kernels for 0%

commit v1 on v0

v1 whole, which is shorter than its diff:
```python
import jax, jax.numpy as jnp, functools
from jax import lax
from jax.experimental import pallas as pl
from jax.experimental.pallas import tpu as pltpu
from jax.sharding import PartitionSpec as P

D = 384
FF = 1536
HEADS = 6
HEAD_DIM = 64
TOK = 197
TP = 208
G = 2
ROWS = G * TP
MB = 3
STEP = 10
CH = 32
FFC = 384

beta_one = 0.9
beta_two = 0.999
learn_rate = 0.01
decay_rate = 0.05
adam_eps = 1e-08
norm_eps = 1e-06
f32 = jnp.float32
bf16 = jnp.bfloat16

LANES = 128
TILE = 8 * LANES
MATS = ((0, D, 3 * D), (3456, D, D), (4608, D, FF), (9216, FF, D))
VEC_ROW = 13824
FLAT_ROWS = 13860
VMEM_LIMIT = 60 * 2**20


def dot(a, b, ca=1, cb=0):
    return lax.dot_general(a, b, (((ca,), (cb,)), ((), ())), preferred_element_type=f32)


def chunk_rows(shard):
    return ((shard + TILE - 1 + LANES - 1) // LANES + 15) // 16 * 16


def first_tile(shard, d):
    return (shard * d) // TILE


def compute_kernel(n, shard, cap, slots, meta, images, cot, p_images, p_cot, wbuf,
                   block_out, input_grad, p_out, p_grad, gbuf,
                   flat, w_qkv, w_o, w_1, w_2, vecs, g_qkv, g_o, g_1, g_2t, vsum,
                   xin, gin, oout, gout, x_s, n1_s, r1_s, a1_s, qkv_s, prob_s, o_s, m_s, n2_s, r2_s, a2_s,
                   g_s, u_s, act_s, du_s, acc_s, da_s, dm_s, db_s, do_s, dqkv_s, zero_b, zero_f,
                   in_sem, out_sem, zero_sem):
    rows_c = wbuf.shape[1]
    own_first = meta[0]
    own_n = meta[1]
    part_n = meta[2]
    live_n = meta[3]
    items = own_n + part_n
    steps = (items + G - 1) // G

    def fetch(step, slot, do):
        for i in range(G):
            item = jnp.minimum(step * G + i, items - 1)
            is_own = item < own_n

            @pl.when(is_own)
            def _():
                s = own_first + item
                for k, (src, dst) in enumerate(((images, xin), (cot, gin))):
                    c = pltpu.make_async_copy(src.at[s], dst.at[slot, i], in_sem.at[slot, i, k])
                    c.start() if do else c.wait()

            @pl.when(jnp.logical_not(is_own))
            def _():
                s = item - own_n
                for k, (src, dst) in enumerate(((p_images, xin), (p_cot, gin))):
                    c = pltpu.make_async_copy(src.at[s], dst.at[slot, i], in_sem.at[slot, i, k])
                    c.start() if do else c.wait()

    def flush(step, slot, do):
        for i in range(G):
            item = step * G + i
            is_own = item < own_n

            @pl.when(is_own)
            def _():
                s = own_first + item
                for k, (dst, src) in enumerate(((block_out, oout), (input_grad, gout))):
                    c = pltpu.make_async_copy(src.at[slot, i], dst.at[s], out_sem.at[slot, i, k])
                    c.start() if do else c.wait()

            @pl.when(jnp.logical_and(jnp.logical_not(is_own), item < items))
            def _():
                s = item - own_n
                for k, (dst, src) in enumerate(((p_out, oout), (p_grad, gout))):
                    c = pltpu.make_async_copy(src.at[slot, i], dst.at[s], out_sem.at[slot, i, k])
                    c.start() if do else c.wait()

    def zeros_copy(do):
        def one(s, carry):
            a = pltpu.make_async_copy(zero_b, block_out.at[s], zero_sem.at[0])
            b = pltpu.make_async_copy(zero_f, input_grad.at[s], zero_sem.at[1])
            a.start() if do else a.wait()
            b.start() if do else b.wait()
            return carry
        lax.fori_loop(live_n, slots, one, 0)

    fetch(0, 0, True)
    zero_b[...] = jnp.zeros(zero_b.shape, bf16)
    zero_f[...] = jnp.zeros(zero_f.shape, f32)
    zeros_copy(True)
    end = 0
    for d in range(n):
        top = 8 * first_tile(shard, d)
        if d == 0:
            flat[pl.ds(0, rows_c), :] = wbuf[0].astype(f32)
        else:
            shared = min(end - top, rows_c)
            flat[pl.ds(top, shared), :] += wbuf[d, pl.ds(0, shared), :].astype(f32)
            if shared < rows_c:
                flat[pl.ds(top + shared, rows_c - shared), :] = wbuf[d, pl.ds(shared, rows_c - shared), :].astype(f32)
        end = top + rows_c
    for ref, (row, height, width) in zip((w_qkv, w_o, w_1, w_2), MATS):
        blocks = width // LANES
        for j in range(blocks):
            ref[:, j * LANES:(j + 1) * LANES] = flat[pl.ds(row + j, height, stride=blocks), :].astype(bf16)
    for k in range(8):
        for j in range(3):
            vecs[k, j * LANES:(j + 1) * LANES] = flat[VEC_ROW + 3 * k + j, :]
    for j in range(12):
        vecs[8, j * LANES:(j + 1) * LANES] = flat[VEC_ROW + 24 + j, :]
    for ref in (g_qkv, g_o, g_1, g_2t, vsum):
        ref[...] = jnp.zeros(ref.shape, f32)
    for ref in (x_s, g_s):
        ref[...] = jnp.zeros(ref.shape, ref.dtype)

    g1 = vecs[0:1, :D]
    b1 = vecs[1:2, :D]
    g2 = vecs[2:3, :D]
    b2 = vecs[3:4, :D]
    cq = vecs[4:5, :D]
    cv = vecs[5:6, :D]
    co = vecs[6:7, :D]
    c2 = vecs[7:8, :D]

    lane = lax.broadcasted_iota(jnp.int32, (1, LANES), 1)
    low_half = lane < HEAD_DIM

    def colsum(v):
        return jnp.sum(v.reshape(v.shape[0] // 8, 8, v.shape[1]), axis=0)

    def mean(v):
        return jnp.sum(v, axis=-1, keepdims=True) * (1.0 / D)

    def body(step, carry):
        slot = lax.rem(step, 2)
        fetch(step, slot, False)

        @pl.when(step + 1 < steps)
        def _():
            fetch(step + 1, 1 - slot, True)

        for i in range(G):
            live = (step * G + i < items).astype(bf16)
            x_s[pl.ds(i * TP, TOK), :] = xin[slot, i].astype(f32)
            g_s[pl.ds(i * TP, TOK), :] = gin[slot, i] * live
        for r in range(0, ROWS, CH):
            rs = pl.ds(r, CH)
            v = x_s[rs, :]
            c = v - mean(v)
            inv = lax.rsqrt(mean(c * c) + norm_eps)
            nv = c * inv
            n1_s[rs, :] = nv
            r1_s[rs, :] = jnp.broadcast_to(inv, (CH, LANES))
            a1_s[rs, :] = (nv * g1 + b1).astype(bf16)
        a1 = a1_s[...]
        for k, bias in ((0, cq), (1, None), (2, cv)):
            cols = slice(k * D, (k + 1) * D)
            t = dot(a1, w_qkv[:, cols])
            qkv_s[:, cols] = (t if bias is None else t + bias).astype(bf16)
        key_live = lax.broadcasted_iota(jnp.int32, (1, TP), 1) < TOK
        for i in range(G):
            ir = pl.ds(i * TP, TP)
            for p in range(HEADS // 2):
                cols = slice(p * LANES, (p + 1) * LANES)
                q = qkv_s[ir, cols] * 0.125
                k = qkv_s[ir, slice(D + p * LANES, D + (p + 1) * LANES)]
                v = qkv_s[ir, slice(2 * D + p * LANES, 2 * D + (p + 1) * LANES)]
                zero = jnp.zeros_like(q)
                qm = jnp.concatenate([jnp.where(low_half, q, zero), jnp.where(low_half, zero, q)], axis=0)
                s = dot(qm, k, 1, 1)
                s = jnp.where(key_live, s, -1e30)
                e = jnp.exp(s - jnp.max(s, axis=-1, keepdims=True))
                pr = e / jnp.sum(e, axis=-1, keepdims=True)
                prob_s[i * 3 + p] = pr
                o2 = dot(pr.astype(bf16), v)
                o_s[ir, cols] = jnp.where(low_half, o2[:TP], o2[TP:]).astype(bf16)
        m_s[...] = dot(o_s[...], w_o[...])
        for r in range(0, ROWS, CH):
            rs = pl.ds(r, CH)
            v = x_s[rs, :] + m_s[rs, :] + co
            m_s[rs, :] = v
            c = v - mean(v)
            inv = lax.rsqrt(mean(c * c) + norm_eps)
            nv = c * inv
            n2_s[rs, :] = nv
            r2_s[rs, :] = jnp.broadcast_to(inv, (CH, LANES))
            a2_s[rs, :] = (nv * g2 + b2).astype(bf16)
        a2 = a2_s[...]
        gl = g_s[...]
        for j in range(FF // FFC):
            cols = slice(j * FFC, (j + 1) * FFC)
            b = j % 2
            u_s[b] = dot(a2, w_1[:, cols])
            da_s[b] = dot(gl, w_2[cols, :], 1, 1)
            c1 = vecs[8:9, cols]
            tot = None
            for r in range(0, ROWS, CH):
                rs = pl.ds(r, CH)
                u = u_s[b, rs, :] + c1
                phi = 0.5 + 0.5 * lax.erf(u * 0.7071067811865476)
                dens = jnp.exp(u * u * -0.5) * 0.3989422804014327
                act_s[b, rs, :] = (u * phi).astype(bf16)
                du = (da_s[b, rs, :] * (phi + u * dens)).astype(bf16)
                du_s[b, rs, :] = du
                part = colsum(du.astype(f32))
                tot = part if tot is None else tot + part
            vsum[8, :, cols] += tot
            act = act_s[b]
            du = du_s[b]
            if j == 0:
                acc_s[...] = dot(act, w_2[cols, :])
                dm_s[...] = dot(du, w_1[:, cols], 1, 1)
            else:
                acc_s[...] += dot(act, w_2[cols, :])
                dm_s[...] += dot(du, w_1[:, cols], 1, 1)
            g_1[:, cols] += dot(a2, du, 0, 0)
            g_2t[:, cols] += dot(gl, act, 0, 0)
        tg2 = tb2 = tco = tc2 = None
        for r in range(0, ROWS, CH):
            rs = pl.ds(r, CH)
            gw = g_s[rs, :].astype(f32)
            acc_s[rs, :] = m_s[rs, :] + acc_s[rs, :] + c2
            e2 = dm_s[rs, :]
            nv = n2_s[rs, :]
            en = e2 * nv
            eg = e2 * g2
            inv = r2_s[rs, :]
            inv = jnp.concatenate([inv, inv, inv], axis=1)
            dm = gw + inv * (eg - mean(eg) - nv * mean(en * g2))
            dm_s[rs, :] = dm
            db = dm.astype(bf16)
            db_s[rs, :] = db
            sums = (colsum(en), colsum(e2), colsum(db.astype(f32)), colsum(gw))
            if tg2 is None:
                tg2, tb2, tco, tc2 = sums
            else:
                tg2, tb2, tco, tc2 = tg2 + sums[0], tb2 + sums[1], tco + sums[2], tc2 + sums[3]
        vsum[2, :, :D] += tg2
        vsum[3, :, :D] += tb2
        vsum[6, :, :D] += tco
        vsum[7, :, :D] += tc2

        @pl.when(step >= 2)
        def _():
            flush(step - 2, slot, False)

        for i in range(G):
            oout[slot, i] = acc_s[pl.ds(i * TP, TOK), :].astype(bf16)
        db = db_s[...]
        g_o[...] += dot(o_s[...], db, 0, 0)
        do_s[...] = dot(db, w_o[...], 1, 1).astype(bf16)
        for i in range(G):
            ir = pl.ds(i * TP, TP)
            for p in range(HEADS // 2):
                cols = slice(p * LANES, (p + 1) * LANES)
                q = qkv_s[ir, cols] * 0.125
                k = qkv_s[ir, slice(D + p * LANES, D + (p + 1) * LANES)]
                v = qkv_s[ir, slice(2 * D + p * LANES, 2 * D + (p + 1) * LANES)]
                do = do_s[ir, cols]
                zero = jnp.zeros_like(q)
                qm = jnp.concatenate([jnp.where(low_half, q, zero), jnp.where(low_half, zero, q)], axis=0)
                dom = jnp.concatenate([jnp.where(low_half, do, zero), jnp.where(low_half, zero, do)], axis=0)
                pr = prob_s[i * 3 + p]
                dp = dot(dom, v, 1, 1)
                delta = jnp.sum(pr * dp, axis=-1, keepdims=True)
                ds = (pr * (dp - delta)).astype(bf16)
                dv = dot(pr.astype(bf16), dom, 0, 0)
                dk = dot(ds, qm, 0, 0)
                dq2 = dot(ds, k * 0.125)
                dq = jnp.where(low_half, dq2[:TP], dq2[TP:])
                dqkv_s[ir, cols] = dq.astype(bf16)
                dqkv_s[ir, slice(D + p * LANES, D + (p + 1) * LANES)] = dk.astype(bf16)
                dqkv_s[ir, slice(2 * D + p * LANES, 2 * D + (p + 1) * LANES)] = dv.astype(bf16)
        dqkv = dqkv_s[...]
        acc_s[...] = dot(dqkv, w_qkv[...], 1, 1)
        g_qkv[...] += dot(a1_s[...], dqkv, 0, 0)
        tg1 = tb1 = tcq = tcv = None
        for r in range(0, ROWS, CH):
            rs = pl.ds(r, CH)
            e1 = acc_s[rs, :]
            nv = n1_s[rs, :]
            en = e1 * nv
            eg = e1 * g1
            inv = r1_s[rs, :]
            inv = jnp.concatenate([inv, inv, inv], axis=1)
            dm_s[rs, :] += inv * (eg - mean(eg) - nv * mean(en * g1))
            sums = (colsum(en), colsum(e1), colsum(dqkv_s[rs, :D].astype(f32)), colsum(dqkv_s[rs, 2 * D:].astype(f32)))
            if tg1 is None:
                tg1, tb1, tcq, tcv = sums
            else:
                tg1, tb1, tcq, tcv = tg1 + sums[0], tb1 + sums[1], tcq + sums[2], tcv + sums[3]
        vsum[0, :, :D] += tg1
        vsum[1, :, :D] += tb1
        vsum[4, :, :D] += tcq
        vsum[5, :, :D] += tcv
        for i in range(G):
            gout[slot, i] = dm_s[pl.ds(i * TP, TOK), :]
        flush(step, slot, True)
        return carry

    lax.fori_loop(0, steps, body, 0)

    for ref, (row, height, width) in zip((g_qkv, g_o, g_1), MATS):
        blocks = width // LANES
        for j in range(blocks):
            flat[pl.ds(row + j, height, stride=blocks), :] = ref[:, j * LANES:(j + 1) * LANES]
    row = MATS[3][0]
    for c in range(FF // LANES):
        t = g_2t[:, c * LANES:(c + 1) * LANES].T
        for j in range(3):
            flat[pl.ds(row + 3 * LANES * c + j, LANES, stride=3), :] = t[:, j * LANES:(j + 1) * LANES]
    for k in range(9):
        t = jnp.sum(vsum[k], axis=0, keepdims=True)
        for j in range(12 if k == 8 else 3):
            flat[pl.ds(VEC_ROW + 3 * k + j, 1), :] = t[:, j * LANES:(j + 1) * LANES]
    flat[pl.ds(FLAT_ROWS, flat.shape[0] - FLAT_ROWS), :] = jnp.zeros((flat.shape[0] - FLAT_ROWS, LANES), f32)
    for d in range(n):
        gbuf[d] = flat[pl.ds(8 * first_tile(shard, d), rows_c), :].astype(bf16)

    @pl.when(steps >= 2)
    def _():
        flush(steps - 2, lax.rem(steps, 2), False)
    flush(steps - 1, lax.rem(steps + 1, 2), False)
    zeros_copy(False)


def flat_height(n, shard):
    return 8 * first_tile(shard, n - 1) + chunk_rows(shard)


def block_call(n, shard, cap, meta, images, cot, p_images, p_cot, wbuf):
    slots = images.shape[0]
    anyspace = pl.BlockSpec(memory_space=pl.ANY)
    vm = pl.BlockSpec(memory_space=pltpu.VMEM)
    rows_c = chunk_rows(shard)
    scratch = [
        pltpu.VMEM((flat_height(n, shard), LANES), f32),
        pltpu.VMEM((D, 3 * D), bf16), pltpu.VMEM((D, D), bf16), pltpu.VMEM((D, FF), bf16), pltpu.VMEM((FF, D), bf16),
        pltpu.VMEM((16, FF), f32),
        pltpu.VMEM((D, 3 * D), f32), pltpu.VMEM((D, D), f32), pltpu.VMEM((D, FF), f32), pltpu.VMEM((D, FF), f32),
        pltpu.VMEM((9, 8, FF), f32),
        pltpu.VMEM((2, G, TOK, D), bf16), pltpu.VMEM((2, G, TOK, D), bf16),
        pltpu.VMEM((2, G, TOK, D), bf16), pltpu.VMEM((2, G, TOK, D), f32),
        pltpu.VMEM((ROWS, D), f32),
        pltpu.VMEM((ROWS, D), f32), pltpu.VMEM((ROWS, LANES), f32), pltpu.VMEM((ROWS, D), bf16),
        pltpu.VMEM((ROWS, 3 * D), bf16),
        pltpu.VMEM((G * 3, 2 * TP, TP), f32),
        pltpu.VMEM((ROWS, D), bf16),
        pltpu.VMEM((ROWS, D), f32),
        pltpu.VMEM((ROWS, D), f32), pltpu.VMEM((ROWS, LANES), f32), pltpu.VMEM((ROWS, D), bf16),
        pltpu.VMEM((ROWS, D), bf16),
        pltpu.VMEM((2, ROWS, FFC), f32), pltpu.VMEM((2, ROWS, FFC), bf16), pltpu.VMEM((2, ROWS, FFC), bf16),
        pltpu.VMEM((ROWS, D), f32),
        pltpu.VMEM((2, ROWS, FFC), f32),
        pltpu.VMEM((ROWS, D), f32), pltpu.VMEM((ROWS, D), bf16), pltpu.VMEM((ROWS, D), bf16),
        pltpu.VMEM((ROWS, 3 * D), bf16),
        pltpu.VMEM((TOK, D), bf16), pltpu.VMEM((TOK, D), f32),
        pltpu.SemaphoreType.DMA((2, G, 2)), pltpu.SemaphoreType.DMA((2, G, 2)), pltpu.SemaphoreType.DMA((2,)),
    ]
    return pl.pallas_call(
        functools.partial(compute_kernel, n, shard, cap, slots),
        name="block",
        out_shape=(
            jax.ShapeDtypeStruct(images.shape, bf16),
            jax.ShapeDtypeStruct(images.shape, f32),
            jax.ShapeDtypeStruct((cap,) + images.shape[1:], bf16),
            jax.ShapeDtypeStruct((cap,) + images.shape[1:], f32),
            jax.ShapeDtypeStruct((n, rows_c, LANES), bf16),
        ),
        in_specs=[pl.BlockSpec(memory_space=pltpu.SMEM), anyspace, anyspace, anyspace, anyspace, vm],
        out_specs=(anyspace, anyspace, anyspace, anyspace, vm),
        scratch_shapes=scratch,
        compiler_params=pltpu.CompilerParams(vmem_limit_bytes=VMEM_LIMIT),
    )(meta, images, cot, p_images, p_cot, wbuf)


def pack_shard(n, shard, values):
    me = lax.axis_index("dp")
    offset = lax.rem(shard * me, TILE)
    padded = lax.dynamic_update_slice_in_dim(jnp.zeros((chunk_rows(shard) * LANES,), values.dtype), values, offset, 0)
    return padded.reshape(chunk_rows(shard), LANES)


def unpack_shard(n, shard, chunk):
    me = lax.axis_index("dp")
    offset = lax.rem(shard * me, TILE)
    return lax.dynamic_slice_in_dim(chunk.reshape(-1), offset, shard, 0)


def body(n, images, cotangent, master, moment_one, moment_two, batch_ends):
    shard = master.shape[0]
    cap = 2
    live_n = batch_ends[0, MB - 1]
    chunk = pack_shard(n, shard, master.astype(bf16))
    wbuf = lax.all_gather(chunk, "dp", axis=0)
    zero = jnp.zeros((), jnp.int32)
    meta = jnp.stack([zero, live_n, zero, live_n])
    block_out, input_grad, p_out, p_grad, gbuf = block_call(n, shard, cap, meta, images, cotangent, images[:cap], cotangent[:cap], wbuf)
    part = lax.psum_scatter(gbuf.astype(f32), "dp", scatter_dimension=0, tiled=False)
    weight_grad = unpack_shard(n, shard, part)
    first_moment = beta_one * moment_one + (1.0 - beta_one) * weight_grad
    second_moment = beta_two * moment_two + (1.0 - beta_two) * weight_grad * weight_grad
    corrected_one = first_moment / (1.0 - beta_one**STEP)
    corrected_two = second_moment / (1.0 - beta_two**STEP)
    update = -learn_rate * (corrected_one / (jnp.sqrt(corrected_two) + adam_eps) + decay_rate * master)
    return (block_out, input_grad, weight_grad, first_moment, second_moment, update)


def solution(mesh):
    n = mesh.shape["dp"]
    return jax.shard_map(
        functools.partial(body, n),
        mesh=mesh,
        in_specs=(P("dp", None, None), P("dp", None, None), P("dp"), P("dp"), P("dp"), P("dp", None)),
        out_specs=(P("dp", None, None), P("dp", None, None), P("dp"), P("dp"), P("dp"), P("dp")),
        check_vma=False,
    )
```

time: 1000 us -> 390 us (0.39)
  matrix products: 341 us -> 0 us
  local copies, waits for them, and re-layouts: 272 us -> 21.5 us
  other arithmetic: 140 us -> 10 us
  Pallas kernels: 0 us -> 85.2 us
  waiting for transfers between devices: 214 us -> 253 us
    dot_general x54 -> x0, matrix products: 341 us -> none  [the longest x3 77.1 us: forward_pass(): jnp.dot(normed_two_low, w_up, preferred_element_type=jnp.float32) + bias_up]
    unnamed x4 -> x2, waiting for transfers between devices: 214 us -> 0.03 us
    reduce_scatter x0 -> x1, waiting for transfers between devices: none -> 197 us  [body(): lax.psum_scatter(gbuf.astype(f32), 'dp', scatter_dimension=0, tiled=False)]
    reshape x28 -> x0, local copies, waits for them, and re-layouts: 156 us -> none  [the longest x6 70 us: forward_pass(): qkv_low.reshape(count_img, TOK_IMG, 3, HEADS, HEAD_DIM)]
    pallas_call x0 -> x1, Pallas kernels: none -> 85.2 us  [block_call(): pl.pallas_call(functools.partial(compute_kernel, n, shard, cap, slots), n...]
    all_gather x0 -> x1, waiting for transfers between devices: none -> 55.4 us  [body(): wbuf = lax.all_gather(chunk, 'dp', axis=0)]
    reduce_sum x16 -> x0, other arithmetic: 53.9 us -> none  [the longest x2 19.1 us: layer_norm(): centered = values - centre]
    convert_element_type x18 -> x0, local copies, waits for them, and re-layouts: 47.4 us -> none  [the longest x6 18.8 us: forward_pass(): rows_in = batch_images.reshape(count_img * TOK_IMG, D).astype(jnp.float32)]
  transfers between devices with their start and end apart: 2 -> 2, of which waited for: 2 -> 2; matrix products, arithmetic and copies ran while one was open for 8% -> 5% of each run, Pallas kernels for 0% -> 0%
where the time goes in v1:
time: 390 us; the launch traced here: 384 us
  waiting for transfers between devices  253 us (65%)
  Pallas kernels  85.2 us (22%)
  local copies, waits for them, and re-layouts  21.5 us (6%)
  between operations  14.1 us (4%)
  other arithmetic  10 us (3%)
    reduce_scatter x1, waiting for transfers between devices, body(): lax.psum_scatter(gbuf.astype(f32), 'dp', scatter_dimension=0, tiled=False)  197 us
    pallas_call x1, Pallas kernels, block_call(): pl.pallas_call(functools.partial(compute_kernel, n, shard, cap, slots), n...  85.2 us
    all_gather x1, waiting for transfers between devices, body(): wbuf = lax.all_gather(chunk, 'dp', axis=0)  55.4 us
    unnamed x18, local copies, waits for them, and re-layouts  17.4 us
  transfers between devices with their start and end apart: 2, of which 2 were waited for; matrix products, arithmetic and copies ran while one was open for 5% of the time, Pallas kernels for 0%

profile of v1, /device:TPU:0, one launch (start us, length us, event | category | flops | bytes accessed | tf_op | source)
XLA Modules:
  0.0 383.6 jit_solution(6290561388655679890)
XLA Ops:
  7.2 0.0 all-gather.2.cloned.1.call-start
  7.2 1.0 convert_element_type.6
  8.2 1.1 dynamic_update_slice.3
  9.4 0.0 copy-start.4
  9.4 0.6 copy-done.4
  10.0 0.0 all-gather.2.cloned.1.call-update
  10.0 0.0 reduce-scatter.2.cloned.1.call-start
  10.1 1.2 slice.9
  11.3 0.0 copy-start.2
  11.3 2.7 copy.20.images
  14.0 0.0 copy-start
  14.0 0.9 slice.12.p_images
  14.8 0.0 copy-done.2
  14.8 0.5 copy.21.cot
  15.3 0.6 copy-done
  15.9 0.0 copy-start.1
  15.9 0.8 slice.13.p_cot
  16.7 1.1 copy-done.1
  17.8 1.2 pad_add_fusion.meta
  19.1 55.4 %all-gather.2.cloned.1.call-done.wbuf = bf16[32,448,128]{2,1,0:T(8,128)(2,1)} async-done(((bf16[1,448,128]{2,1,0:T(8,128)(2,1)}), bf16[32,448,128]{2,1,0:T(8,128)(2,1)}) %all-gather.2.cloned.1.call-update) | async-done | bytes 3670032 | tf_op jit(solution)/shard_map/all_gather | solution.py:418
  74.5 85.2 %block.1 = (bf16[24,197,384]{2,1,0:T(8,128)(2,1)}, f32[24,197,384]{2,1,0:T(8,128)}, bf16[2,197,384]{2,1,0:T(8,128)(2,1)}, f32[2,197,384]{2,1,0:T(8,128)}, bf16[32,448,128]{2,1,0:T(8,128)(2,1)}) custom-call(s32[4]{0:T(128)} %pad_add_fusion.meta, bf16[24,197,384]{2,1,0:T(8,128)(2,1)} %copy-done, bf16[24,197,384]{2,1,0:T(8,128)(2,1)} %copy-done.1, ...), custom_call_target="tpu_custom_call" | custom-call | tf_op jit(solution)/shard_map/block/pallas_call | solution.py:383
  159.7 5.8 %convert_element_type.7 = f32[32,448,128]{2,1,0:T(8,128)} convert(bf16[32,448,128]{2,1,0:T(8,128)(2,1)} %get-tuple-element.11) | non-fusion elementwise | flops 1835008 | bytes 11010048 | tf_op jit(solution)/shard_map/convert_element_type | solution.py:422
  165.6 0.0 reduce-scatter.2.cloned.1.call-update
  165.6 4.3 %copy.22 = bf16[24,197,384]{2,0,1:T(8,128)(2,1)} copy(bf16[24,197,384]{2,1,0:T(8,128)(2,1)} %get-tuple-element.18) | data formatting | bytes 7262208
  169.9 0.0 copy-start.3
  169.9 0.0 copy-start.5
  169.9 0.0 copy-start.6
  169.9 7.6 %copy.23 = f32[24,197,384]{2,0,1:T(8,128)} copy(f32[24,197,384]{2,1,0:T(8,128)} %get-tuple-element.19) | data formatting | bytes 14524416
  177.5 197.2 %reduce-scatter.2.cloned.1.call-done = f32[1,448,128]{2,1,0:T(8,128)} async-done(((f32[32,448,128]{2,1,0:T(8,128)}), f32[1,448,128]{2,1,0:T(8,128)}) %reduce-scatter.2.cloned.1.call-update) | async-done | bytes 229392 | tf_op jit(solution)/shard_map/reduce_scatter | solution.py:422
  374.7 0.0 copy-done.3
  374.7 0.0 copy-done.5
  374.7 0.0 copy-done.6
  374.7 2.0 add_multiply_fusion
  (1 shorter events, 0.0 us)
Async XLA Ops:
  7.2 67.3 %all-gather.2.cloned.1.call-start = ((), (), s32[]{:S(2)}) async-start(), calls=%async_computation.1 | async-start | bytes 3784704 | tf_op jit(solution)/shard_map/all_gather | solution.py:418
  9.4 0.6 copy-start.4
  10.0 364.7 %reduce-scatter.2.cloned.1.call-start = ((), (), s32[]{:S(2)}) async-start(), calls=%async_computation.2 | async-start | bytes 7569408 | tf_op jit(solution)/shard_map/reduce_scatter | solution.py:422
  11.3 3.5 copy-start.2
  14.0 1.9 copy-start
  15.9 1.9 copy-start.1
  169.9 204.8 %copy-start.3 = (f32[55440]{0:T(1024)S(1)}, f32[55440]{0:T(1024)}, u32[]{:S(2)}) copy-start(f32[55440]{0:T(1024)} %param.8) | copy-start | bytes 665284
  169.9 204.8 %copy-start.5 = (f32[55440]{0:T(1024)S(1)}, f32[55440]{0:T(1024)}, u32[]{:S(2)}) copy-start(f32[55440]{0:T(1024)} %param.10) | copy-start | bytes 665284
  169.9 204.8 %copy-start.6 = (f32[55440]{0:T(1024)S(1)}, f32[55440]{0:T(1024)}, u32[]{:S(2)}) copy-start(f32[55440]{0:T(1024)} %param.9) | copy-start | bytes 665284
Sparse Core Ops, SparseCore 0:
  11.4 63.0 all-gather.1
  165.7 208.9 reduce-scatter.1
